TPU v7x, 32 devices: a whole 2x2x4 slice. The times are simulated.
32 devices in a mesh: tm: 16 (over z, y, x), space: 2 (over core).
Axes of the slice: x: 2, y: 2, z: 4, core: 2. Of those that a mesh axis runs over, the one named last changes fastest.
Arguments:
- snapshots: float32 [4096, 3, 1024], P('tm', None, 'space'), may hold values from -108 to 108
- weights: float32 [1024], P('space'), may hold values from 0.1 to 1
- start: float32 [2, 15, 8], replicated, may hold values from -6 to 6
Outputs:
- mode_out: float32 [64, 8, 2, 3, 1024], P('tm', None, None, None, 'space')
- energy: float32 [64, 8], P('tm')
All inputs are finite; a program needn't handle non-finite values.
Results may differ from a plain program's by a relative error of at most 0.0003.
Values sent between devices are 32-bit elements; how exact they have to be, the bound alone decides.
A program may use at most 64 MiB of HBM per device.

v0:
```python
import math
import jax
import jax.numpy as jnp
from jax import lax
from jax.sharding import PartitionSpec as P

NF = 64
ITERS = 8
precise = lax.Precision.HIGHEST
epsilon = 1e-06


def shifted(block, axis, distance):
    devices = range(lax.axis_size(axis))
    route = [(i - distance, i) for i in devices if i - distance in devices]
    return lax.ppermute(block, axis, route)


def dft_table(freqs, seg_len):
    length = 2 * seg_len
    times = jnp.arange(length, dtype=jnp.int32)
    freq_ids = jnp.arange(freqs, dtype=jnp.int32)
    turns = jnp.mod(freq_ids[:, None] * times[None, :], length).astype(jnp.float32)
    phase = 2.0 * math.pi / length * turns
    window = 0.5 - 0.5 * jnp.cos(2.0 * math.pi / length * times.astype(jnp.float32))
    factor = 1.0 / jnp.sqrt(jnp.sum(window * window))
    return jnp.concatenate([window * jnp.cos(phase) * factor, -window * jnp.sin(phase) * factor], 0)


def gram_parts(spectra, col_weights, total_points):
    weighted = spectra * col_weights
    grams = jnp.einsum("nrfc,msfc->frnsm", spectra, weighted, precision=precise)
    gram_re = (grams[:, 0, :, 0, :] + grams[:, 1, :, 1, :]) / total_points
    gram_im = (grams[:, 0, :, 1, :] - grams[:, 1, :, 0, :]) / total_points
    return (gram_re, gram_im)


def apply_gram(gram_re, gram_im, vec_re, vec_im):
    img_re = jnp.einsum("fnm,fmk->fnk", gram_re, vec_re, precision=precise) - jnp.einsum(
        "fnm,fmk->fnk", gram_im, vec_im, precision=precise
    )
    img_im = jnp.einsum("fnm,fmk->fnk", gram_re, vec_im, precision=precise) + jnp.einsum(
        "fnm,fmk->fnk", gram_im, vec_re, precision=precise
    )
    return (img_re, img_im)


def orthonormal(img_re, img_im):
    cols_re = []
    cols_im = []
    for column in range(img_re.shape[-1]):
        part_re = img_re[..., column]
        part_im = img_im[..., column]
        if column > 0:
            prev_re = jnp.stack(cols_re, -1)
            prev_im = jnp.stack(cols_im, -1)
            for repeat in range(2):
                coef_re = jnp.sum(
                    prev_re * part_re[..., None] + prev_im * part_im[..., None], axis=1
                )
                coef_im = jnp.sum(
                    prev_re * part_im[..., None] - prev_im * part_re[..., None], axis=1
                )
                part_re = part_re - jnp.sum(
                    prev_re * coef_re[:, None, :] - prev_im * coef_im[:, None, :], axis=-1
                )
                part_im = part_im - jnp.sum(
                    prev_re * coef_im[:, None, :] + prev_im * coef_re[:, None, :], axis=-1
                )
        inverse = 1.0 / jnp.sqrt(jnp.sum(part_re * part_re + part_im * part_im, axis=1) + epsilon)
        cols_re.append(part_re * inverse[:, None])
        cols_im.append(part_im * inverse[:, None])
    return (jnp.stack(cols_re, -1), jnp.stack(cols_im, -1))


def subspace(gram_re, gram_im, start):
    shape = (gram_re.shape[0], start.shape[1], start.shape[2])
    vec_re = jnp.broadcast_to(start[0], shape)
    vec_im = jnp.broadcast_to(start[1], shape)
    for sweep in range(ITERS):
        img_re, img_im = apply_gram(gram_re, gram_im, vec_re, vec_im)
        vec_re, vec_im = orthonormal(img_re, img_im)
    return (vec_re, vec_im)


def project(spectra, vec_re, vec_im):
    real_rows = spectra[:, 0]
    imag_rows = spectra[:, 1]
    mode_re = jnp.einsum("nfc,fnk->fkc", real_rows, vec_re, precision=precise) - jnp.einsum(
        "nfc,fnk->fkc", imag_rows, vec_im, precision=precise
    )
    mode_im = jnp.einsum("nfc,fnk->fkc", real_rows, vec_im, precision=precise) + jnp.einsum(
        "nfc,fnk->fkc", imag_rows, vec_re, precision=precise
    )
    return (mode_re, mode_im)


def body(snapshots, weights, start):
    seg_len, components, points = snapshots.shape
    columns = components * points
    samples = snapshots.reshape(seg_len, columns)
    basis = dft_table(NF, seg_len)
    tm_count = lax.axis_size("tm")
    blocks = tm_count - 1
    later = shifted(samples, "tm", -1)
    window_rows = jnp.concatenate([samples, later], 0)
    spectrum = jnp.dot(basis, window_rows, precision=precise)
    arrived = lax.all_to_all(
        spectrum.reshape(1, 2, NF, columns), "tm", split_axis=2, concat_axis=0, tiled=True
    )
    spectra = arrived[:blocks]
    col_weights = jnp.tile(weights, components)
    total_points = points * lax.axis_size("space")
    gram_re, gram_im = gram_parts(spectra, col_weights, total_points)
    gram_re, gram_im = lax.psum((gram_re, gram_im), "space")
    vec_re, vec_im = subspace(gram_re, gram_im, start)
    mode_re, mode_im = project(spectra, vec_re, vec_im)
    partial_energy = (
        jnp.sum((mode_re * mode_re + mode_im * mode_im) * col_weights, axis=-1) / total_points
    )
    energy = lax.psum(partial_energy, "space")
    inverse = 1.0 / jnp.sqrt(energy + epsilon)
    mode_out = jnp.stack([mode_re, mode_im], 2) * inverse[:, :, None, None]
    freq_count = mode_out.shape[0]
    return (mode_out.reshape(freq_count, mode_out.shape[1], 2, components, points), energy)


def solution(mesh):
    in_specs = (P("tm", None, "space"), P("space"), P())
    out_specs = (P("tm", None, None, None, "space"), P("tm", None))
    return jax.shard_map(body, mesh=mesh, in_specs=in_specs, out_specs=out_specs, check_vma=False)
```

profile of v0, /device:TPU:0, one launch (start us, length us, event | category | flops | bytes accessed | tf_op | source)
XLA Modules:
  0.0 132.0 jit_solution(17040012056975748923)
XLA Ops:
  0.6 1.9 %copy.460 = f32[256,3,512]{0,2,1:T(8,128)S(1)} copy(f32[256,3,512]{2,0,1:T(8,128)} %param.3) | data formatting | bytes 3145728 | tf_op args[0]
  2.5 1.3 collective-permute-start
  3.8 0.6 multiply_reduce_fusion.1
  5.2 0.5 multiply_multiply_fusion
  5.8 35.9 %collective-permute-done = f32[256,1536]{0,1:T(8,128)S(1)} collective-permute-done((f32[256,1536]{0,1:T(8,128)S(1)}, f32[256,1536]{0,1:T(8,128)S(1)}, u32[]{:S(2)}, u32[]{:S(2)}) %collective-permute-start) | collective-permute-done | bytes 1572896 | tf_op jit(solution)/shard_map/ppermute | solution.py:16
  41.7 3.3 %fusion = f32[128,1536]{1,0:T(8,128)S(1)} fusion(f32[256,1536]{0,1:T(8,128)S(1)} %collective-permute-done, f32[256,1536]{0,1:T(8,128)S(1)} %bitcast.878, f32[64,512]{1,0:T(8,128)S(1)} %get-tuple-element.722, f32[64,512]{1,0:T(8,128)S(1)} %get-tuple-element.723), kind=kOutput, calls=%fused_computation | convolution fusion | flops 1208811520 | bytes 4194304 | tf_op jit(solution)/shard_map/dot_general | solution.py:107
  45.1 1.5 %copy.461 = f32[1,2,64,1536]{3,1,0,2:T(2,128)} copy(f32[1,2,64,1536]{3,2,1,0:T(8,128)S(1)} %bitcast.879) | data formatting | bytes 1572864 | tf_op jit(solution)/shard_map/reshape | solution.py:109
  46.6 7.9 %all-to-all-start = ((f32[1,2,64,1536]{3,1,0,2:T(2,128)}), f32[1,2,64,1536]{3,1,0,2:T(2,128)S(1)}, u32[]{:S(2)}, u32[]{:S(2)}) async-start(f32[1,2,64,1536]{3,1,0,2:T(2,128)} %copy.461), calls=%async_computation | async-start | bytes 1572864 | tf_op jit(solution)/shard_map/all_to_all | solution.py:108
  54.5 18.8 %all-to-all-done = f32[1,2,64,1536]{3,1,0,2:T(2,128)S(1)} async-done(((f32[1,2,64,1536]{3,1,0,2:T(2,128)}), f32[1,2,64,1536]{3,1,0,2:T(2,128)S(1)}, u32[]{:S(2)}, u32[]{:S(2)}) %all-to-all-start) | async-done | bytes 786464 | tf_op jit(solution)/shard_map/all_to_all | solution.py:108
  73.4 0.5 copy.724
  73.9 3.4 %convolution_bitcast_fusion = f32[4,2,15,2,15]{2,4,1,3,0:T(8,128)S(1)} fusion(f32[16,1,2,4,1536]{4,0,2,3,1:T(8,128)S(1)} %bitcast.876, f32[1536]{0:T(1024)S(1)} %mul.8264), kind=kOutput, calls=%fused_computation.6 | convolution fusion | flops 66539520 | bytes 1595456 | tf_op jit(solution)/shard_map/nrfc,msfc->frnsm/dot_general | solution.py:32
  77.3 3.8 %all-reduce = (f32[4,15,15]{1,2,0:T(8,128)S(1)}, f32[4,15,15]{1,2,0:T(8,128)S(1)}) all-reduce(f32[4,15,15]{1,2,0:T(8,128)S(1)} %get-tuple-element.477, f32[4,15,15]{1,2,0:T(8,128)S(1)} %get-tuple-element.476), channel_id=1, replica_groups=mesh['tm'=16,'space'=2] {'space'}, use_global_device_ids=true, to_apply=%region_1.2 | all-reduce | flops 1800 | bytes 14400 | tf_op jit(solution)/shard_map/psum | solution.py:115
  81.9 0.2 add_reduce_fusion.270
  82.1 0.2 add_reduce_fusion.269
  82.3 0.2 add_reduce_fusion.268
  87.1 0.2 convolution_subtract_fusion.7
  87.6 0.2 add_reduce_fusion.260
  87.7 0.2 add_reduce_fusion.259
  87.9 0.2 add_reduce_fusion.258
  92.7 0.2 convolution_subtract_fusion.6
  93.2 0.2 add_reduce_fusion.250
  93.4 0.2 add_reduce_fusion.249
  93.6 0.2 add_reduce_fusion.248
  98.4 0.2 convolution_subtract_fusion.5
  98.9 0.2 add_reduce_fusion.240
  99.1 0.2 add_reduce_fusion.239
  99.2 0.2 add_reduce_fusion.238
  104.5 0.2 add_reduce_fusion.230
  104.7 0.2 add_reduce_fusion.229
  104.9 0.2 add_reduce_fusion.228
  109.7 0.2 convolution_subtract_fusion.3
  110.2 0.2 add_reduce_fusion.220
  110.4 0.2 add_reduce_fusion.219
  110.6 0.2 add_reduce_fusion.218
  116.1 0.2 add_reduce_fusion.210
  116.2 0.2 add_reduce_fusion.209
  116.4 0.2 add_reduce_fusion.208
  121.7 0.2 add_reduce_fusion.200
  121.9 0.2 add_reduce_fusion.199
  122.1 0.2 add_reduce_fusion.198
  126.6 0.3 fusion.9
  126.9 0.3 fusion.10
  127.2 0.3 convolution_subtract_fusion
  127.6 0.4 multiply_reduce_fusion
  128.0 0.2 copy.688
  128.2 2.5 %psum.23 = f32[4,8]{1,0:T(4,128)S(1)} all-reduce(f32[4,8]{1,0:T(4,128)S(1)} %broadcast_multiply_fusion), channel_id=1, replica_groups=mesh['tm'=16,'space'=2] {'space'}, use_global_device_ids=true, to_apply=%region_484.485 | all-reduce | flops 32 | bytes 256 | tf_op jit(solution)/shard_map/psum | solution.py:121
  130.7 0.2 copy.687
  130.9 1.1 maximum_multiply_fusion
  (571 shorter events, 38.7 us)
Async XLA Ops:
  2.5 39.2 %collective-permute-start = (f32[256,1536]{0,1:T(8,128)S(1)}, f32[256,1536]{0,1:T(8,128)S(1)}, u32[]{:S(2)}, u32[]{:S(2)}) collective-permute-start(f32[256,1536]{0,1:T(8,128)S(1)} %bitcast.877), channel_id=1, source_target_pairs={{2,0},{4,2},{6,4},{8,6},{10,8},{12,10},{14,12},{16,14},{18,16},{20... | collective-permute-start | bytes 4718600 | tf_op jit(solution)/shard_map/ppermute | solution.py:16
  45.1 9.4 %copy-start.2 = (f32[512]{0:T(512)S(1)}, f32[512]{0:T(512)}, u32[]{:S(2)}) copy-start(f32[512]{0:T(512)} %param.4) | copy-start | bytes 6148
  45.1 9.4 %copy-start = (f32[2,15,8]{1,2,0:T(8,128)S(1)}, f32[2,15,8]{1,2,0:T(8,128)}, u32[]{:S(2)}) copy-start(f32[2,15,8]{1,2,0:T(8,128)} %param.5) | copy-start | bytes 2884
  46.6 26.8 %all-to-all-start = ((f32[1,2,64,1536]{3,1,0,2:T(2,128)}), f32[1,2,64,1536]{3,1,0,2:T(2,128)S(1)}, u32[]{:S(2)}, u32[]{:S(2)}) async-start(f32[1,2,64,1536]{3,1,0,2:T(2,128)} %copy.461), calls=%async_computation | async-start | bytes 1572864 | tf_op jit(solution)/shard_map/all_to_all | solution.py:108
  130.7 1.3 %copy-start.1 = (f32[4,8]{1,0:T(4,128)}, f32[4,8]{1,0:T(4,128)S(1)}, u32[]{:S(2)}) copy-start(f32[4,8]{1,0:T(4,128)S(1)} %psum.23) | copy-start | bytes 388
where the time goes:
time: 132 us
  waiting for transfers between devices  54.8 us (42%)
  other arithmetic  38.5 us (29%)
  matrix products  13.4 us (10%)
  starting transfers between devices  9.18 us (7%)
  local copies, waits for them, and re-layouts  6.57 us (5%)
  blocking collectives  6.25 us (5%)
  between operations  3.29 us (2%)
    ppermute x1, waiting for transfers between devices, shifted(): return lax.ppermute(block, axis, route)  35.9 us
    all_to_all x1, waiting for transfers between devices, body(): lax.all_to_all(spectrum.reshape(1, 2, NF, columns), 'tm', split_axis=2, c...  18.8 us
    reduce_sum x112, other arithmetic, orthonormal(): jnp.sum(prev_re * part_re[..., None] + prev_im * part_im[..., None], axis=1)  13 us
    reduce_sum x96, other arithmetic, orthonormal(): jnp.sum(prev_re * coef_re[:, None, :] - prev_im * coef_im[:, None, :], ax...  9.33 us
    reduce_sum x64, other arithmetic, orthonormal(): jnp.sum(part_re * part_re + part_im * part_im, axis=1) + epsilon  8.27 us
    all_to_all x1, starting transfers between devices, body(): lax.all_to_all(spectrum.reshape(1, 2, NF, columns), 'tm', split_axis=2, c...  7.89 us
    mul x56, other arithmetic, orthonormal(): cols_re.append(part_re * inverse[:, None])  4.27 us
    psum x1, blocking collectives, body(): gram_re, gram_im = lax.psum((gram_re, gram_im), 'space')  3.78 us
  transfers between devices with their start and end apart: 2, of which 2 were waited for; matrix products, arithmetic and copies ran while one was open for 1% of the time, Pallas kernels for 0%

commit v1 on v0

--- a/solution.py
+++ b/solution.py
@@ -8,6 +8,17 @@
 ITERS = 8
 precise = lax.Precision.HIGHEST
 epsilon = 1e-06
+
+
+def cut_along(x, dim, peers):
+    before, after = (x.shape[:dim], x.shape[dim + 1 :])
+    return jnp.moveaxis(x.reshape(*before, peers, -1, *after), dim, 0)
+
+
+def laid_out(pieces, dim):
+    pieces = jnp.moveaxis(pieces, 0, dim)
+    shape = pieces.shape
+    return pieces.reshape(*shape[:dim], shape[dim] * shape[dim + 1], *shape[dim + 2 :])
 
 
 def shifted(block, axis, distance):
@@ -105,9 +116,15 @@
     later = shifted(samples, "tm", -1)
     window_rows = jnp.concatenate([samples, later], 0)
     spectrum = jnp.dot(basis, window_rows, precision=precise)
-    arrived = lax.all_to_all(
-        spectrum.reshape(1, 2, NF, columns), "tm", split_axis=2, concat_axis=0, tiled=True
-    )
+    shard = spectrum.reshape(1, 2, NF, columns)
+    length_2, index = (lax.axis_size("tm"), lax.axis_index("tm"))
+    blocks_2 = cut_along(shard, 2, length_2)
+    outs = [blocks_2[index]]
+    for lap in range(1, length_2):
+        sent = blocks_2[index ^ lap]
+        outs.append(lax.ppermute(sent, "tm", [(i_2, i_2 ^ lap) for i_2 in range(length_2)]))
+    blocks_2 = jnp.stack(outs)[index ^ jnp.arange(length_2)]
+    arrived = laid_out(blocks_2, 0)
     spectra = arrived[:blocks]
     col_weights = jnp.tile(weights, components)
     total_points = points * lax.axis_size("space")

time: 132 us -> 143 us (1.083)
  starting transfers between devices: 9.18 us -> 30.2 us
  waiting for transfers between devices: 54.8 us -> 42 us
  matrix products: 13.4 us -> 15.7 us
    ppermute x0 -> x15, starting transfers between devices: none -> 28.9 us  [body(): lax.ppermute(sent, 'tm', [(i_2, i_2 ^ lap) for i_2 in range(length_2)])]
    all_to_all x1 -> x0, waiting for transfers between devices: 18.8 us -> none  [body(): lax.all_to_all(spectrum.reshape(1, 2, NF, columns), 'tm', split_axis=2, c...]
    all_to_all x1 -> x0, starting transfers between devices: 7.89 us -> none  [body(): lax.all_to_all(spectrum.reshape(1, 2, NF, columns), 'tm', split_axis=2, c...]
    ppermute x0 -> x15, waiting for transfers between devices: none -> 6.13 us  [body(): lax.ppermute(sent, 'tm', [(i_2, i_2 ^ lap) for i_2 in range(length_2)])]
    reshape x1 -> x0, local copies, waits for them, and re-layouts: 1.48 us -> none  [body(): spectrum.reshape(1, 2, NF, columns)]
  transfers between devices with their start and end apart: 2 -> 16, of which waited for: 2 -> 3; matrix products, arithmetic and copies ran while one was open for 1% -> 1% of each run, Pallas kernels for 0% -> 0%
where the time goes in v1:
time: 143 us
  waiting for transfers between devices  42 us (29%)
  other arithmetic  38.6 us (27%)
  starting transfers between devices  30.2 us (21%)
  matrix products  15.7 us (11%)
  local copies, waits for them, and re-layouts  6.26 us (4%)
  blocking collectives  6.25 us (4%)
  between operations  3.63 us (3%)
    ppermute x1, waiting for transfers between devices, shifted(): return lax.ppermute(block, axis, route)  35.8 us
    ppermute x15, starting transfers between devices, body(): lax.ppermute(sent, 'tm', [(i_2, i_2 ^ lap) for i_2 in range(length_2)])  28.9 us
    reduce_sum x112, other arithmetic, orthonormal(): jnp.sum(prev_re * part_re[..., None] + prev_im * part_im[..., None], axis=1)  13 us
    reduce_sum x96, other arithmetic, orthonormal(): jnp.sum(prev_re * coef_re[:, None, :] - prev_im * coef_im[:, None, :], ax...  9.33 us
    reduce_sum x64, other arithmetic, orthonormal(): jnp.sum(part_re * part_re + part_im * part_im, axis=1) + epsilon  8.27 us
    ppermute x15, waiting for transfers between devices, body(): lax.ppermute(sent, 'tm', [(i_2, i_2 ^ lap) for i_2 in range(length_2)])  6.13 us
    dot_general x1, matrix products, body(): spectrum = jnp.dot(basis, window_rows, precision=precise)  4.73 us
    mul x56, other arithmetic, orthonormal(): cols_re.append(part_re * inverse[:, None])  4.27 us
  transfers between devices with their start and end apart: 16, of which 3 were waited for; matrix products, arithmetic and copies ran while one was open for 1% of the time, Pallas kernels for 0%

profile of v1, /device:TPU:0, one launch (start us, length us, event | category | flops | bytes accessed | tf_op | source)
XLA Modules:
  0.0 142.5 jit_solution(12416514388657872448)
XLA Ops:
  0.7 1.9 %copy.231 = f32[256,3,512]{0,2,1:T(8,128)S(1)} copy(f32[256,3,512]{2,0,1:T(8,128)} %param.3) | data formatting | bytes 3145728 | tf_op args[0]
  2.5 1.3 collective-permute-start
  3.9 0.6 multiply_reduce_fusion.1
  5.5 0.5 multiply_multiply_fusion
  6.1 35.8 %collective-permute-done = f32[256,1536]{0,1:T(8,128)} collective-permute-done((f32[256,1536]{0,1:T(8,128)S(1)}, f32[256,1536]{0,1:T(8,128)}, u32[]{:S(2)}, u32[]{:S(2)}) %collective-permute-start) | collective-permute-done | bytes 1572896 | tf_op jit(solution)/shard_map/ppermute | solution.py:27
  41.9 4.7 %fusion = f32[128,1536]{1,0:T(8,128)S(1)} fusion(f32[256,1536]{0,1:T(8,128)} %collective-permute-done, f32[256,1536]{0,1:T(8,128)S(1)} %bitcast.931, f32[64,512]{1,0:T(8,128)S(1)} %get-tuple-element.739, f32[64,512]{1,0:T(8,128)S(1)} %get-tuple-element.740), kind=kOutput, calls=%fused_computation.1 | convolution fusion | flops 1208811520 | bytes 4194304 | tf_op jit(solution)/shard_map/dot_general | solution.py:118
  46.6 0.2 reshape_reshape.3
  46.9 0.2 dynamic-slice_bitcast_fusion
  47.1 2.7 %collective-permute-start.1 = (f32[1,2,4,1536]{3,2,1,0:T(4,128)S(1)}, f32[1,2,4,1536]{3,2,1,0:T(4,128)S(1)}, u32[]{:S(2)}, u32[]{:S(2)}) collective-permute-start(f32[1,2,4,1536]{3,2,1,0:T(4,128)S(1)} %get-tuple-element.492), channel_id=1, source_target_pairs={{0,2},{2,0},{4,6},{6,4},{8,10},{10,8},{12,14},{14,12},{16,18},{18,... | collective-permute-start | bytes 147464 | tf_op jit(solution)/shard_map/ppermute | solution.py:125
  49.8 2.4 %collective-permute-start.2 = (f32[1,2,4,1536]{3,2,1,0:T(4,128)S(1)}, f32[1,2,4,1536]{3,2,1,0:T(4,128)S(1)}, u32[]{:S(2)}, u32[]{:S(2)}) collective-permute-start(f32[1,2,4,1536]{3,2,1,0:T(4,128)S(1)} %get-tuple-element.491), channel_id=1, source_target_pairs={{0,4},{2,6},{4,0},{6,2},{8,12},{10,14},{12,8},{14,10},{16,20},{18,... | collective-permute-start | bytes 147464 | tf_op jit(solution)/shard_map/ppermute | solution.py:125
  52.2 1.6 %collective-permute-start.4 = (f32[1,2,4,1536]{3,2,1,0:T(4,128)S(1)}, f32[1,2,4,1536]{3,2,1,0:T(4,128)S(1)}, u32[]{:S(2)}, u32[]{:S(2)}) collective-permute-start(f32[1,2,4,1536]{3,2,1,0:T(4,128)S(1)} %get-tuple-element.489), channel_id=1, source_target_pairs={{0,8},{2,10},{4,12},{6,14},{8,0},{10,2},{12,4},{14,6},{16,24},{18,... | collective-permute-start | bytes 147464 | tf_op jit(solution)/shard_map/ppermute | solution.py:125
  53.8 1.4 collective-permute-start.5
  55.2 3.0 %collective-permute-start.6 = (f32[1,2,4,1536]{3,2,1,0:T(4,128)S(1)}, f32[1,2,4,1536]{3,2,1,0:T(4,128)S(1)}, u32[]{:S(2)}, u32[]{:S(2)}) collective-permute-start(f32[1,2,4,1536]{3,2,1,0:T(4,128)S(1)} %get-tuple-element.487), channel_id=1, source_target_pairs={{0,12},{2,14},{4,8},{6,10},{8,4},{10,6},{12,0},{14,2},{16,28},{18,... | collective-permute-start | bytes 147464 | tf_op jit(solution)/shard_map/ppermute | solution.py:125
  58.3 2.5 %collective-permute-start.8 = (f32[1,2,4,1536]{3,2,1,0:T(4,128)S(1)}, f32[1,2,4,1536]{3,2,1,0:T(4,128)S(1)}, u32[]{:S(2)}, u32[]{:S(2)}) collective-permute-start(f32[1,2,4,1536]{3,2,1,0:T(4,128)S(1)} %get-tuple-element.485), channel_id=1, source_target_pairs={{0,16},{2,18},{4,20},{6,22},{8,24},{10,26},{12,28},{14,30},{16,0},... | collective-permute-start | bytes 147464 | tf_op jit(solution)/shard_map/ppermute | solution.py:125
  60.8 1.4 collective-permute-start.9
  62.3 4.0 %collective-permute-start.10 = (f32[1,2,4,1536]{3,2,1,0:T(4,128)S(1)}, f32[1,2,4,1536]{3,2,1,0:T(4,128)S(1)}, u32[]{:S(2)}, u32[]{:S(2)}) collective-permute-start(f32[1,2,4,1536]{3,2,1,0:T(4,128)S(1)} %get-tuple-element.483), channel_id=1, source_target_pairs={{0,20},{2,22},{4,16},{6,18},{8,28},{10,30},{12,24},{14,26},{16,4},... | collective-permute-start | bytes 147464 | tf_op jit(solution)/shard_map/ppermute | solution.py:125
  66.4 2.6 %collective-permute-start.12 = (f32[1,2,4,1536]{3,2,1,0:T(4,128)S(1)}, f32[1,2,4,1536]{3,2,1,0:T(4,128)S(1)}, u32[]{:S(2)}, u32[]{:S(2)}) collective-permute-start(f32[1,2,4,1536]{3,2,1,0:T(4,128)S(1)} %get-tuple-element.481), channel_id=1, source_target_pairs={{0,24},{2,26},{4,28},{6,30},{8,16},{10,18},{12,20},{14,22},{16,8},... | collective-permute-start | bytes 147464 | tf_op jit(solution)/shard_map/ppermute | solution.py:125
  69.0 2.3 %collective-permute-start.13 = (f32[1,2,4,1536]{3,2,1,0:T(4,128)S(1)}, f32[1,2,4,1536]{3,2,1,0:T(4,128)S(1)}, u32[]{:S(2)}, u32[]{:S(2)}) collective-permute-start(f32[1,2,4,1536]{3,2,1,0:T(4,128)S(1)} %get-tuple-element.480), channel_id=1, source_target_pairs={{0,26},{2,24},{4,30},{6,28},{8,18},{10,16},{12,22},{14,20},{16,10}... | collective-permute-start | bytes 147464 | tf_op jit(solution)/shard_map/ppermute | solution.py:125
  71.3 3.3 %collective-permute-start.14 = (f32[1,2,4,1536]{3,2,1,0:T(4,128)S(1)}, f32[1,2,4,1536]{3,2,1,0:T(4,128)S(1)}, u32[]{:S(2)}, u32[]{:S(2)}) collective-permute-start(f32[1,2,4,1536]{3,2,1,0:T(4,128)S(1)} %get-tuple-element.479), channel_id=1, source_target_pairs={{0,28},{2,30},{4,24},{6,26},{8,20},{10,22},{12,16},{14,18},{16,12}... | collective-permute-start | bytes 147464 | tf_op jit(solution)/shard_map/ppermute | solution.py:125
  74.6 1.5 %collective-permute-start.15 = (f32[1,2,4,1536]{3,2,1,0:T(4,128)S(1)}, f32[1,2,4,1536]{3,2,1,0:T(4,128)S(1)}, u32[]{:S(2)}, u32[]{:S(2)}) collective-permute-start(f32[1,2,4,1536]{3,2,1,0:T(4,128)S(1)} %get-tuple-element.478), channel_id=1, source_target_pairs={{0,30},{2,28},{4,26},{6,24},{8,22},{10,20},{12,18},{14,16},{16,14}... | collective-permute-start | bytes 147464 | tf_op jit(solution)/shard_map/ppermute | solution.py:125
  76.3 2.0 %collective-permute-done.14 = f32[1,2,4,1536]{3,2,1,0:T(4,128)S(1)} collective-permute-done((f32[1,2,4,1536]{3,2,1,0:T(4,128)S(1)}, f32[1,2,4,1536]{3,2,1,0:T(4,128)S(1)}, u32[]{:S(2)}, u32[]{:S(2)}) %collective-permute-start.14) | collective-permute-done | bytes 49184 | tf_op jit(solution)/shard_map/ppermute | solution.py:125
  78.3 4.1 %collective-permute-done.15 = f32[1,2,4,1536]{3,2,1,0:T(4,128)S(1)} collective-permute-done((f32[1,2,4,1536]{3,2,1,0:T(4,128)S(1)}, f32[1,2,4,1536]{3,2,1,0:T(4,128)S(1)}, u32[]{:S(2)}, u32[]{:S(2)}) %collective-permute-start.15) | collective-permute-done | bytes 49184 | tf_op jit(solution)/shard_map/ppermute | solution.py:125
  82.4 1.0 gather_fusion
  83.5 3.8 %convolution_bitcast_fusion = f32[4,2,15,2,15]{2,4,1,3,0:T(8,128)S(1)} fusion(f32[15,2,4,1536]{3,2,1,0:T(4,128)S(1)} %slice.557, f32[1536]{0:T(1024)S(1)} %mul.8264), kind=kOutput, calls=%fused_computation.7 | convolution fusion | flops 66539520 | bytes 757824 | tf_op jit(solution)/shard_map/nrfc,msfc->frnsm/dot_general | solution.py:43
  87.3 3.8 %all-reduce = (f32[4,15,15]{1,2,0:T(8,128)S(1)}, f32[4,15,15]{1,2,0:T(8,128)S(1)}) all-reduce(f32[4,15,15]{1,2,0:T(8,128)S(1)} %get-tuple-element.494, f32[4,15,15]{1,2,0:T(8,128)S(1)} %get-tuple-element.493), channel_id=1, replica_groups=mesh['tm'=16,'space'=2] {'space'}, use_global_device_ids=true, to_apply=%region_1.2 | all-reduce | flops 1800 | bytes 14400 | tf_op jit(solution)/shard_map/psum | solution.py:132
  91.9 0.2 add_reduce_fusion.270
  92.1 0.2 add_reduce_fusion.269
  97.6 0.2 add_reduce_fusion.260
  97.8 0.2 add_reduce_fusion.259
  103.2 0.2 add_reduce_fusion.250
  103.4 0.2 add_reduce_fusion.249
  108.9 0.2 add_reduce_fusion.240
  109.1 0.2 add_reduce_fusion.239
  114.5 0.2 add_reduce_fusion.230
  114.7 0.2 add_reduce_fusion.229
  120.2 0.2 add_reduce_fusion.220
  120.4 0.2 add_reduce_fusion.219
  126.1 0.2 add_reduce_fusion.210
  126.3 0.2 add_reduce_fusion.209
  131.9 0.2 add_reduce_fusion.199
  136.6 0.4 fusion.10
  137.0 0.4 fusion.9
  137.5 0.4 convolution_subtract_fusion
  137.9 0.5 multiply_reduce_fusion
  138.5 0.2 copy.460
  138.7 0.2 copy.459
  138.9 2.5 %psum.23 = f32[4,8]{1,0:T(4,128)S(1)} all-reduce(f32[4,8]{1,0:T(4,128)S(1)} %broadcast_multiply_fusion), channel_id=1, replica_groups=mesh['tm'=16,'space'=2] {'space'}, use_global_device_ids=true, to_apply=%region_484.485 | all-reduce | flops 32 | bytes 256 | tf_op jit(solution)/shard_map/psum | solution.py:138
  141.4 1.1 maximum_multiply_fusion
  (619 shorter events, 41.4 us)
Async XLA Ops:
  0.6 4.6 %copy-start.2 = (f32[512]{0:T(512)S(1)}, f32[512]{0:T(512)}, u32[]{:S(2)}) copy-start(f32[512]{0:T(512)} %param.4) | copy-start | bytes 6148
  0.6 4.8 %copy-start = (f32[2,15,8]{1,2,0:T(8,128)S(1)}, f32[2,15,8]{1,2,0:T(8,128)}, u32[]{:S(2)}) copy-start(f32[2,15,8]{1,2,0:T(8,128)} %param.5) | copy-start | bytes 2884
  2.5 39.3 %collective-permute-start = (f32[256,1536]{0,1:T(8,128)S(1)}, f32[256,1536]{0,1:T(8,128)}, u32[]{:S(2)}, u32[]{:S(2)}) collective-permute-start(f32[256,1536]{0,1:T(8,128)S(1)} %bitcast.930), channel_id=1, source_target_pairs={{2,0},{4,2},{6,4},{8,6},{10,8},{12,10},{14,12},{16,14},{18,16},{20... | collective-permute-start | bytes 4718600 | tf_op jit(solution)/shard_map/ppermute | solution.py:27
  47.1 8.1 %collective-permute-start.1 = (f32[1,2,4,1536]{3,2,1,0:T(4,128)S(1)}, f32[1,2,4,1536]{3,2,1,0:T(4,128)S(1)}, u32[]{:S(2)}, u32[]{:S(2)}) collective-permute-start(f32[1,2,4,1536]{3,2,1,0:T(4,128)S(1)} %get-tuple-element.492), channel_id=1, source_target_pairs={{0,2},{2,0},{4,6},{6,4},{8,10},{10,8},{12,14},{14,12},{16,18},{18,... | collective-permute-start | bytes 147464 | tf_op jit(solution)/shard_map/ppermute | solution.py:125
  49.8 8.4 %collective-permute-start.2 = (f32[1,2,4,1536]{3,2,1,0:T(4,128)S(1)}, f32[1,2,4,1536]{3,2,1,0:T(4,128)S(1)}, u32[]{:S(2)}, u32[]{:S(2)}) collective-permute-start(f32[1,2,4,1536]{3,2,1,0:T(4,128)S(1)} %get-tuple-element.491), channel_id=1, source_target_pairs={{0,4},{2,6},{4,0},{6,2},{8,12},{10,14},{12,8},{14,10},{16,20},{18,... | collective-permute-start | bytes 147464 | tf_op jit(solution)/shard_map/ppermute | solution.py:125
  52.2 6.1 %collective-permute-start.3 = (f32[1,2,4,1536]{3,2,1,0:T(4,128)S(1)}, f32[1,2,4,1536]{3,2,1,0:T(4,128)S(1)}, u32[]{:S(2)}, u32[]{:S(2)}) collective-permute-start(f32[1,2,4,1536]{3,2,1,0:T(4,128)S(1)} %get-tuple-element.490), channel_id=1, source_target_pairs={{0,6},{2,4},{4,2},{6,0},{8,14},{10,12},{12,10},{14,8},{16,22},{18,... | collective-permute-start | bytes 147464 | tf_op jit(solution)/shard_map/ppermute | solution.py:125
  52.2 8.6 %collective-permute-start.4 = (f32[1,2,4,1536]{3,2,1,0:T(4,128)S(1)}, f32[1,2,4,1536]{3,2,1,0:T(4,128)S(1)}, u32[]{:S(2)}, u32[]{:S(2)}) collective-permute-start(f32[1,2,4,1536]{3,2,1,0:T(4,128)S(1)} %get-tuple-element.489), channel_id=1, source_target_pairs={{0,8},{2,10},{4,12},{6,14},{8,0},{10,2},{12,4},{14,6},{16,24},{18,... | collective-permute-start | bytes 147464 | tf_op jit(solution)/shard_map/ppermute | solution.py:125
  53.8 8.5 %collective-permute-start.5 = (f32[1,2,4,1536]{3,2,1,0:T(4,128)S(1)}, f32[1,2,4,1536]{3,2,1,0:T(4,128)S(1)}, u32[]{:S(2)}, u32[]{:S(2)}) collective-permute-start(f32[1,2,4,1536]{3,2,1,0:T(4,128)S(1)} %get-tuple-element.488), channel_id=1, source_target_pairs={{0,10},{2,8},{4,14},{6,12},{8,2},{10,0},{12,6},{14,4},{16,26},{18,... | collective-permute-start | bytes 147464 | tf_op jit(solution)/shard_map/ppermute | solution.py:125
  55.2 11.1 %collective-permute-start.6 = (f32[1,2,4,1536]{3,2,1,0:T(4,128)S(1)}, f32[1,2,4,1536]{3,2,1,0:T(4,128)S(1)}, u32[]{:S(2)}, u32[]{:S(2)}) collective-permute-start(f32[1,2,4,1536]{3,2,1,0:T(4,128)S(1)} %get-tuple-element.487), channel_id=1, source_target_pairs={{0,12},{2,14},{4,8},{6,10},{8,4},{10,6},{12,0},{14,2},{16,28},{18,... | collective-permute-start | bytes 147464 | tf_op jit(solution)/shard_map/ppermute | solution.py:125
  58.2 8.2 %collective-permute-start.7 = (f32[1,2,4,1536]{3,2,1,0:T(4,128)S(1)}, f32[1,2,4,1536]{3,2,1,0:T(4,128)S(1)}, u32[]{:S(2)}, u32[]{:S(2)}) collective-permute-start(f32[1,2,4,1536]{3,2,1,0:T(4,128)S(1)} %get-tuple-element.486), channel_id=1, source_target_pairs={{0,14},{2,12},{4,10},{6,8},{8,6},{10,4},{12,2},{14,0},{16,30},{18,... | collective-permute-start | bytes 147464 | tf_op jit(solution)/shard_map/ppermute | solution.py:125
  58.3 10.7 %collective-permute-start.8 = (f32[1,2,4,1536]{3,2,1,0:T(4,128)S(1)}, f32[1,2,4,1536]{3,2,1,0:T(4,128)S(1)}, u32[]{:S(2)}, u32[]{:S(2)}) collective-permute-start(f32[1,2,4,1536]{3,2,1,0:T(4,128)S(1)} %get-tuple-element.485), channel_id=1, source_target_pairs={{0,16},{2,18},{4,20},{6,22},{8,24},{10,26},{12,28},{14,30},{16,0},... | collective-permute-start | bytes 147464 | tf_op jit(solution)/shard_map/ppermute | solution.py:125
  60.8 10.5 %collective-permute-start.9 = (f32[1,2,4,1536]{3,2,1,0:T(4,128)S(1)}, f32[1,2,4,1536]{3,2,1,0:T(4,128)S(1)}, u32[]{:S(2)}, u32[]{:S(2)}) collective-permute-start(f32[1,2,4,1536]{3,2,1,0:T(4,128)S(1)} %get-tuple-element.484), channel_id=1, source_target_pairs={{0,18},{2,16},{4,22},{6,20},{8,26},{10,24},{12,30},{14,28},{16,2},... | collective-permute-start | bytes 147464 | tf_op jit(solution)/shard_map/ppermute | solution.py:125
  62.3 12.3 %collective-permute-start.10 = (f32[1,2,4,1536]{3,2,1,0:T(4,128)S(1)}, f32[1,2,4,1536]{3,2,1,0:T(4,128)S(1)}, u32[]{:S(2)}, u32[]{:S(2)}) collective-permute-start(f32[1,2,4,1536]{3,2,1,0:T(4,128)S(1)} %get-tuple-element.483), channel_id=1, source_target_pairs={{0,20},{2,22},{4,16},{6,18},{8,28},{10,30},{12,24},{14,26},{16,4},... | collective-permute-start | bytes 147464 | tf_op jit(solution)/shard_map/ppermute | solution.py:125
  66.3 9.9 %collective-permute-start.11 = (f32[1,2,4,1536]{3,2,1,0:T(4,128)S(1)}, f32[1,2,4,1536]{3,2,1,0:T(4,128)S(1)}, u32[]{:S(2)}, u32[]{:S(2)}) collective-permute-start(f32[1,2,4,1536]{3,2,1,0:T(4,128)S(1)} %get-tuple-element.482), channel_id=1, source_target_pairs={{0,22},{2,20},{4,18},{6,16},{8,30},{10,28},{12,26},{14,24},{16,6},... | collective-permute-start | bytes 147464 | tf_op jit(solution)/shard_map/ppermute | solution.py:125
  66.4 9.8 %collective-permute-start.12 = (f32[1,2,4,1536]{3,2,1,0:T(4,128)S(1)}, f32[1,2,4,1536]{3,2,1,0:T(4,128)S(1)}, u32[]{:S(2)}, u32[]{:S(2)}) collective-permute-start(f32[1,2,4,1536]{3,2,1,0:T(4,128)S(1)} %get-tuple-element.481), channel_id=1, source_target_pairs={{0,24},{2,26},{4,28},{6,30},{8,16},{10,18},{12,20},{14,22},{16,8},... | collective-permute-start | bytes 147464 | tf_op jit(solution)/shard_map/ppermute | solution.py:125
  69.0 7.3 %collective-permute-start.13 = (f32[1,2,4,1536]{3,2,1,0:T(4,128)S(1)}, f32[1,2,4,1536]{3,2,1,0:T(4,128)S(1)}, u32[]{:S(2)}, u32[]{:S(2)}) collective-permute-start(f32[1,2,4,1536]{3,2,1,0:T(4,128)S(1)} %get-tuple-element.480), channel_id=1, source_target_pairs={{0,26},{2,24},{4,30},{6,28},{8,18},{10,16},{12,22},{14,20},{16,10}... | collective-permute-start | bytes 147464 | tf_op jit(solution)/shard_map/ppermute | solution.py:125
  71.3 7.0 %collective-permute-start.14 = (f32[1,2,4,1536]{3,2,1,0:T(4,128)S(1)}, f32[1,2,4,1536]{3,2,1,0:T(4,128)S(1)}, u32[]{:S(2)}, u32[]{:S(2)}) collective-permute-start(f32[1,2,4,1536]{3,2,1,0:T(4,128)S(1)} %get-tuple-element.479), channel_id=1, source_target_pairs={{0,28},{2,30},{4,24},{6,26},{8,20},{10,22},{12,16},{14,18},{16,12}... | collective-permute-start | bytes 147464 | tf_op jit(solution)/shard_map/ppermute | solution.py:125
  74.6 7.8 %collective-permute-start.15 = (f32[1,2,4,1536]{3,2,1,0:T(4,128)S(1)}, f32[1,2,4,1536]{3,2,1,0:T(4,128)S(1)}, u32[]{:S(2)}, u32[]{:S(2)}) collective-permute-start(f32[1,2,4,1536]{3,2,1,0:T(4,128)S(1)} %get-tuple-element.478), channel_id=1, source_target_pairs={{0,30},{2,28},{4,26},{6,24},{8,22},{10,20},{12,18},{14,16},{16,14}... | collective-permute-start | bytes 147464 | tf_op jit(solution)/shard_map/ppermute | solution.py:125
  141.4 1.1 copy-start.1
